TPU v7x, 128 devices: a whole 4x4x4 slice. The times are simulated.
128 devices in a mesh: heads: 4 (over x), docs: 32 (over z, y, core).
Axes of the slice: x: 4, y: 4, z: 4, core: 2. Of those that a mesh axis runs over, the one named last changes fastest.
Arguments:
- query_rows: bfloat16 [16384, 4096], P('docs', 'heads'), may hold values from -40 to 40
- key_rows: bfloat16 [16384, 512], P('docs', 'heads'), may hold values from -4.5 to 4.5
- value_rows: bfloat16 [16384, 512], P('docs', 'heads'), may hold values from -6 to 6
- doc_blocks: int32 [16], replicated, may hold values from 1 to 16, 128 in all
- out_weight: bfloat16 [4096, 2048], P('heads', 'docs'), may hold values from -0.1875 to 0.1875
Outputs:
- mixed: bfloat16 [16384, 2048], P('docs', 'heads')
All inputs are finite; a program needn't handle non-finite values.
Results may differ from a plain program's by a relative error of at most 0.0095.
Values may be sent and summed in bfloat16 or wider, within the bound.
A program may use at most 64 MiB of HBM per device.

v0:
```python
import jax
import jax.numpy as jnp
from jax import lax
from jax.sharding import PartitionSpec as P

HD = 128
BLOCK = 128
MOSTB = 16


def from_behind(block, axis, distance):
    devices = range(lax.axis_size(axis))
    route = [(i - distance, i) for i in devices if i - distance in devices]
    return lax.ppermute(block, axis, route)


def cut_along(value, dim, size):
    lengths = value.shape
    parts = value.reshape(*lengths[:dim], size, lengths[dim] // size, *lengths[dim + 1 :])
    return jnp.moveaxis(parts, dim, 0)


def summed_on_arrival(value, axis, dim):
    parts = cut_along(value, dim, lax.axis_size(axis))
    arrived = lax.all_to_all(parts, axis, split_axis=0, concat_axis=0, tiled=True)
    return arrived.astype(jnp.float32).sum(axis=0)


def local(query_rows, key_rows, value_rows, doc_blocks, out_weight):
    local_tokens = query_rows.shape[0]
    head_size = key_rows.shape[1]
    first_token = lax.axis_index("docs") * local_tokens
    reach = (MOSTB - 1) * BLOCK
    shard_count = (reach + local_tokens - 1) // local_tokens
    key_pieces = []
    value_pieces = []
    for distance in range(shard_count, 0, -1):
        tail_pair = jnp.stack([key_rows, value_rows])
        before = from_behind(tail_pair, "docs", distance)
        key_pieces.append(before[0])
        value_pieces.append(before[1])
    ext_keys = jnp.concatenate(key_pieces + [key_rows], axis=0)
    ext_values = jnp.concatenate(value_pieces + [value_rows], axis=0)
    rim_rows = ext_keys.shape[0] - local_tokens
    doc_ends = jnp.cumsum(doc_blocks) * BLOCK
    positions = first_token - rim_rows + jnp.arange(rim_rows + local_tokens, dtype=jnp.int32)
    doc_ids = jnp.sum((doc_ends[None, :] <= positions[:, None]).astype(jnp.int32), axis=1)
    doc_ids = jnp.where(positions < 0, -1, doc_ids)
    query_block = min(512, local_tokens)
    window = reach + query_block
    offset = rim_rows - reach
    heads_here = query_rows.shape[1] // head_size
    head_pack = min(4, heads_here)
    pack_count = heads_here // head_pack
    block_count = local_tokens // query_block
    score_scale = HD ** (-0.5)

    def one_block(block_index):
        block_number = block_index // pack_count
        pack_index = block_index % pack_count
        first_row = block_number * query_block
        query_part = lax.dynamic_slice(
            query_rows,
            (first_row, pack_index * head_pack * head_size),
            (query_block, head_pack * head_size),
        ).reshape(query_block, head_pack, head_size)
        key_window = lax.dynamic_slice_in_dim(ext_keys, first_row + offset, window, 0)
        value_window = lax.dynamic_slice_in_dim(ext_values, first_row + offset, window, 0)
        query_doc = lax.dynamic_slice_in_dim(doc_ids, first_row + rim_rows, query_block, 0)
        key_doc = lax.dynamic_slice_in_dim(doc_ids, first_row + offset, window, 0)
        query_pos = first_row + rim_rows + jnp.arange(query_block, dtype=jnp.int32)
        key_pos = first_row + offset + jnp.arange(window, dtype=jnp.int32)
        allowed = (query_doc[:, None] == key_doc[None, :]) & (
            key_pos[None, :] <= query_pos[:, None]
        )
        scores = (
            jnp.einsum("qhd,kd->hqk", query_part, key_window, preferred_element_type=jnp.float32)
            * score_scale
        )
        scores = jnp.where(allowed[None], scores, -jnp.inf)
        row_max = jnp.max(scores, axis=-1, keepdims=True)
        raised = jnp.exp(scores - row_max)
        row_sum = jnp.sum(raised, axis=-1)
        probs = raised.astype(jnp.bfloat16)
        mixed = jnp.einsum("hqk,kd->qhd", probs, value_window, preferred_element_type=jnp.float32)
        mixed = mixed / jnp.transpose(row_sum)[:, :, None]
        return mixed.astype(jnp.bfloat16).reshape(query_block, head_pack * head_size)

    blocks = lax.map(one_block, jnp.arange(block_count * pack_count, dtype=jnp.int32))
    attended = blocks.reshape(block_count, pack_count, query_block, head_pack * head_size)
    attended = jnp.transpose(attended, (0, 2, 1, 3)).reshape(local_tokens, heads_here * head_size)
    partial_value = jnp.dot(
        attended,
        lax.all_gather(out_weight, "docs", axis=1, tiled=True),
        preferred_element_type=jnp.float32,
    )
    summed = summed_on_arrival(partial_value.astype(jnp.bfloat16), "heads", 1)
    return summed.astype(jnp.bfloat16)


def solution(mesh):
    placed = (P("docs", "heads"), P("docs", "heads"), P("docs", "heads"), P(), P("heads", "docs"))
    return jax.shard_map(
        local, mesh=mesh, in_specs=placed, out_specs=P("docs", "heads"), check_vma=False
    )
```

profile of v0, /device:TPU:1, one launch (start us, length us, event | category | flops | bytes accessed | tf_op | source)
XLA Modules:
  0.0 119.8 jit_solution(16681318204415916620)
XLA Ops:
  6.5 0.0 all-gather.2.cloned.1.call-start
  6.5 1.0 pad_maximum_fusion
  7.5 5.7 %collective-permute-start = (bf16[2,512,128]{2,1,0:T(8,128)(2,1)S(1)}, bf16[2,512,128]{2,1,0:T(8,128)(2,1)S(1)}, u32[]{:S(2)}, u32[]{:S(2)}) collective-permute-start(bf16[2,512,128]{2,1,0:T(8,128)(2,1)S(1)} %pad_maximum_fusion), channel_id=1, source_target_pairs={{0,4},{1,5},{2,6},{3,7},{4,8},{5,9},{6,10},{7,11},{8,12},{9,13},{1... | collective-permute-start | bytes 786440 | tf_op jit(solution)/shard_map/ppermute | solution.py:14
  13.2 4.2 %collective-permute-start.1 = (bf16[2,512,128]{2,1,0:T(8,128)(2,1)S(1)}, bf16[2,512,128]{2,1,0:T(8,128)(2,1)S(1)}, u32[]{:S(2)}, u32[]{:S(2)}) collective-permute-start(bf16[2,512,128]{2,1,0:T(8,128)(2,1)S(1)} %pad_maximum_fusion), channel_id=1, source_target_pairs={{0,3},{1,4},{2,5},{3,6},{4,7},{5,8},{6,9},{7,10},{8,11},{9,12},{10... | collective-permute-start | bytes 786440 | tf_op jit(solution)/shard_map/ppermute | solution.py:14
  17.4 3.2 %collective-permute-start.2 = (bf16[2,512,128]{2,1,0:T(8,128)(2,1)S(1)}, bf16[2,512,128]{2,1,0:T(8,128)(2,1)S(1)}, u32[]{:S(2)}, u32[]{:S(2)}) collective-permute-start(bf16[2,512,128]{2,1,0:T(8,128)(2,1)S(1)} %pad_maximum_fusion), channel_id=1, source_target_pairs={{0,2},{1,3},{2,4},{3,5},{4,6},{5,7},{6,8},{7,9},{8,10},{9,11},{10,... | collective-permute-start | bytes 786440 | tf_op jit(solution)/shard_map/ppermute | solution.py:14
  20.6 1.9 %collective-permute-start.3 = (bf16[2,512,128]{2,1,0:T(8,128)(2,1)S(1)}, bf16[2,512,128]{2,1,0:T(8,128)(2,1)S(1)}, u32[]{:S(2)}, u32[]{:S(2)}) collective-permute-start(bf16[2,512,128]{2,1,0:T(8,128)(2,1)S(1)} %pad_maximum_fusion), channel_id=1, source_target_pairs={{0,1},{1,2},{2,3},{3,4},{4,5},{5,6},{6,7},{7,8},{8,9},{9,10},{10,1... | collective-permute-start | bytes 786440 | tf_op jit(solution)/shard_map/ppermute | solution.py:14
  22.5 0.0 all-gather.2.cloned.1.call-update
  22.6 0.7 copy.22
  23.3 0.1 multiply_reduce_fusion
  23.4 0.1 convert_reduce_fusion
  23.6 0.0 collective-permute-done
  23.6 0.2 collective-permute-done.1
  23.8 5.6 %collective-permute-done.2 = bf16[2,512,128]{2,1,0:T(8,128)(2,1)S(1)} collective-permute-done((bf16[2,512,128]{2,1,0:T(8,128)(2,1)S(1)}, bf16[2,512,128]{2,1,0:T(8,128)(2,1)S(1)}, u32[]{:S(2)}, u32[]{:S(2)}) %collective-permute-start.2) | collective-permute-done | bytes 262176 | tf_op jit(solution)/shard_map/ppermute | solution.py:14
  29.5 3.9 %collective-permute-done.3 = bf16[2,512,128]{2,1,0:T(8,128)(2,1)S(1)} collective-permute-done((bf16[2,512,128]{2,1,0:T(8,128)(2,1)S(1)}, bf16[2,512,128]{2,1,0:T(8,128)(2,1)S(1)}, u32[]{:S(2)}, u32[]{:S(2)}) %collective-permute-start.3) | collective-permute-done | bytes 262176 | tf_op jit(solution)/shard_map/ppermute | solution.py:14
  33.4 1.0 constant_dynamic-update-slice_fusion.1
  34.5 42.3 %while.12 = (s32[]{:T(128)}, bf16[2,512,512]{1,2,0:T(8,128)(2,1)}, s32[2]{0:T(128)S(1)}, bf16[2560,128]{1,0:T(8,128)(2,1)S(1)}, s32[2560]{0:T(1024)S(1)}, /*inde...) while((s32[]{:T(128)}, bf16[2,512,512]{1,2,0:T(8,128)(2,1)}, ...), condition=%wide.region_5.6_spmd, body=%wide.region_2.5_spmd.sunk | while | flops 2609183744 | bytes 75532880 | solution.py:89
  34.5 0.0 copy-start
  34.5 0.7 dynamic_slice.58
  38.0 0.1 dynamic_slice.60
  38.1 0.1 dynamic_slice.59
  38.2 1.9 %compare_and_fusion.2 = pred[512,2432]{0,1:T(8,128)(4,1)S(1)} fusion(s32[512]{0:T(512)S(1)} %iota_add_fusion.5, s32[512]{0:T(512)S(1)} %dynamic_slice.59, s32[2432]{0:T(1024)S(1)} %iota_add_fusion.6, s32[2432]{0:T(1024)S(1)} %dynamic_slice.60), kind=kLoop, calls=%fused_computation.7.clone.1 | loop fusion | flops 3735552 | bytes 1268736 | tf_op jit(solution)/shard_map/while/body/eval_jaxpr/and | solution.py:73
  40.1 0.0 copy-done
  40.1 1.1 constant_dynamic-slice_fusion.2
  41.2 0.2 copy.34
  41.4 3.5 %fusion.39 = (f32[4,512]{1,0:T(4,128)S(1)}, f32[2432,512,4]{1,0,2:T(8,128)S(1)}) fusion(pred[512,2432]{0,1:T(8,128)(4,1)S(1)} %compare_and_fusion.2, bf16[512,4,128]{0,2,1:T(8,128)(2,1)S(1)} %bitcast.102, bf16[2560,128]{1,0:T(8,128)(2,1)S(1)} %get-tuple-element.241, s32[]{:T(128)S(6)} %select_n.78), kind=kOutput, calls=%fused_computation.4.clone.1 | convolution fusion | flops 1290008576 | bytes 22323204 | tf_op jit(solution)/shard_map/while/body/eval_jaxpr/qhd,kd->hqk/dot_general | solution.py:77
  44.9 0.0 copy-start.1
  44.9 4.4 %fusion.40 = f32[4,512]{1,0:T(4,128)S(1)} fusion(f32[2432,512,4]{1,0,2:T(8,128)S(1)} %get-tuple-element.200, f32[4,512]{1,0:T(4,128)S(1)} %get-tuple-element.201, pred[512,2432]{0,1:T(8,128)(4,1)S(1)} %compare_and_fusion.2), kind=kLoop, calls=%fused_computation.2.clone.1 | loop fusion | flops 19920896 | bytes 21184512 | tf_op jit(solution)/shard_map/while/body/eval_jaxpr/reduce_sum | solution.py:83
  49.3 0.0 copy-done.1
  49.3 5.4 %divide_convert_fusion.2 = bf16[512,4,128]{0,2,1:T(8,128)(2,1)S(1)} fusion(f32[2432,512,4]{1,0,2:T(8,128)S(1)} %get-tuple-element.200, f32[4,512]{1,0:T(4,128)S(1)} %get-tuple-element.201, pred[512,2432]{0,1:T(8,128)(4,1)S(1)} %compare_and_fusion.2, bf16[2560,128]{1,0:T(8,128)(2,1)S(1)} %copy-done.1, s32[]{:T(128)S(6)} %select_n.78, ...), kind=kOutput, calls=%fused_computation.9.clone.1 | convolution fusion | flops 1295515648 | bytes 22331396 | tf_op jit(solution)/shard_map/while/body/eval_jaxpr/hqk,kd->qhd/dot_general | solution.py:85
  54.7 0.8 constant_dynamic-update-slice_fusion.4
  55.6 0.0 copy-start
  55.6 0.7 dynamic_slice.58
  59.1 0.1 dynamic_slice.60
  59.2 0.1 dynamic_slice.59
  59.3 1.9 %compare_and_fusion.2 = pred[512,2432]{0,1:T(8,128)(4,1)S(1)} fusion(s32[512]{0:T(512)S(1)} %iota_add_fusion.5, s32[512]{0:T(512)S(1)} %dynamic_slice.59, s32[2432]{0:T(1024)S(1)} %iota_add_fusion.6, s32[2432]{0:T(1024)S(1)} %dynamic_slice.60), kind=kLoop, calls=%fused_computation.7.clone.1 | loop fusion | flops 3735552 | bytes 1268736 | tf_op jit(solution)/shard_map/while/body/eval_jaxpr/and | solution.py:73
  61.2 0.0 copy-done
  61.2 1.1 constant_dynamic-slice_fusion.2
  62.3 0.2 copy.34
  62.5 3.5 %fusion.39 = (f32[4,512]{1,0:T(4,128)S(1)}, f32[2432,512,4]{1,0,2:T(8,128)S(1)}) fusion(pred[512,2432]{0,1:T(8,128)(4,1)S(1)} %compare_and_fusion.2, bf16[512,4,128]{0,2,1:T(8,128)(2,1)S(1)} %bitcast.102, bf16[2560,128]{1,0:T(8,128)(2,1)S(1)} %get-tuple-element.241, s32[]{:T(128)S(6)} %select_n.78), kind=kOutput, calls=%fused_computation.4.clone.1 | convolution fusion | flops 1290008576 | bytes 22323204 | tf_op jit(solution)/shard_map/while/body/eval_jaxpr/qhd,kd->hqk/dot_general | solution.py:77
  66.0 0.0 copy-start.1
  66.0 4.4 %fusion.40 = f32[4,512]{1,0:T(4,128)S(1)} fusion(f32[2432,512,4]{1,0,2:T(8,128)S(1)} %get-tuple-element.200, f32[4,512]{1,0:T(4,128)S(1)} %get-tuple-element.201, pred[512,2432]{0,1:T(8,128)(4,1)S(1)} %compare_and_fusion.2), kind=kLoop, calls=%fused_computation.2.clone.1 | loop fusion | flops 19920896 | bytes 21184512 | tf_op jit(solution)/shard_map/while/body/eval_jaxpr/reduce_sum | solution.py:83
  70.4 0.0 copy-done.1
  70.4 5.4 %divide_convert_fusion.2 = bf16[512,4,128]{0,2,1:T(8,128)(2,1)S(1)} fusion(f32[2432,512,4]{1,0,2:T(8,128)S(1)} %get-tuple-element.200, f32[4,512]{1,0:T(4,128)S(1)} %get-tuple-element.201, pred[512,2432]{0,1:T(8,128)(4,1)S(1)} %compare_and_fusion.2, bf16[2560,128]{1,0:T(8,128)(2,1)S(1)} %copy-done.1, s32[]{:T(128)S(6)} %select_n.78, ...), kind=kOutput, calls=%fused_computation.9.clone.1 | convolution fusion | flops 1295515648 | bytes 22331396 | tf_op jit(solution)/shard_map/while/body/eval_jaxpr/hqk,kd->qhd/dot_general | solution.py:85
  75.8 0.9 constant_dynamic-update-slice_fusion.4
  76.7 4.9 %convolution_convert_fusion = bf16[512,2048]{1,0:T(8,128)(2,1)S(1)} fusion(bf16[512,1024]{0,1:T(8,128)(2,1)} %bitcast.21, bf16[1024,2048]{0,1:T(8,128)(2,1)} %all-gather.2.cloned.1.call-done), kind=kOutput, calls=%fused_computation.23 | convolution fusion | flops 2148532224 | bytes 7340032 | tf_op jit(solution)/shard_map/dot_general | solution.py:92
  81.6 0.2 copy.32
  81.8 29.9 %all_to_all.5 = bf16[4,512,512]{2,1,0:T(8,128)(2,1)S(1)} all-to-all(bf16[4,512,512]{2,1,0:T(8,128)(2,1)S(1)} %bitcast.104), channel_id=1, replica_groups=mesh['heads'=4,'docs'=32] {'heads'}, dimensions={0} | all-to-all | bytes 4194304 | tf_op jit(solution)/shard_map/all_to_all | solution.py:25
  111.7 1.2 %reduce_sum.34 = bf16[512,512]{1,0:T(8,128)(2,1)} reduce(bf16[4,512,512]{2,1,0:T(8,128)(2,1)S(1)} %all_to_all.5, bf16[]{:T(256)} %constant.114.clone.1), dimensions={0}, to_apply=%region_6.7 | reduce | flops 786432 | bytes 2621442 | tf_op jit(solution)/shard_map/reduce_sum | solution.py:26
  (14 shorter events, 0.2 us)
Async XLA Ops:
  6.5 70.2 %all-gather.2.cloned.1.call-start = ((), (), s32[]{:S(2)}) async-start(), calls=%async_computation.1 | async-start | bytes 4325376 | tf_op jit(solution)/shard_map/all_gather | solution.py:94
  7.5 16.0 %collective-permute-start = (bf16[2,512,128]{2,1,0:T(8,128)(2,1)S(1)}, bf16[2,512,128]{2,1,0:T(8,128)(2,1)S(1)}, u32[]{:S(2)}, u32[]{:S(2)}) collective-permute-start(bf16[2,512,128]{2,1,0:T(8,128)(2,1)S(1)} %pad_maximum_fusion), channel_id=1, source_target_pairs={{0,4},{1,5},{2,6},{3,7},{4,8},{5,9},{6,10},{7,11},{8,12},{9,13},{1... | collective-permute-start | bytes 786440 | tf_op jit(solution)/shard_map/ppermute | solution.py:14
  13.2 10.6 %collective-permute-start.1 = (bf16[2,512,128]{2,1,0:T(8,128)(2,1)S(1)}, bf16[2,512,128]{2,1,0:T(8,128)(2,1)S(1)}, u32[]{:S(2)}, u32[]{:S(2)}) collective-permute-start(bf16[2,512,128]{2,1,0:T(8,128)(2,1)S(1)} %pad_maximum_fusion), channel_id=1, source_target_pairs={{0,3},{1,4},{2,5},{3,6},{4,7},{5,8},{6,9},{7,10},{8,11},{9,12},{10... | collective-permute-start | bytes 786440 | tf_op jit(solution)/shard_map/ppermute | solution.py:14
  17.4 12.1 %collective-permute-start.2 = (bf16[2,512,128]{2,1,0:T(8,128)(2,1)S(1)}, bf16[2,512,128]{2,1,0:T(8,128)(2,1)S(1)}, u32[]{:S(2)}, u32[]{:S(2)}) collective-permute-start(bf16[2,512,128]{2,1,0:T(8,128)(2,1)S(1)} %pad_maximum_fusion), channel_id=1, source_target_pairs={{0,2},{1,3},{2,4},{3,5},{4,6},{5,7},{6,8},{7,9},{8,10},{9,11},{10,... | collective-permute-start | bytes 786440 | tf_op jit(solution)/shard_map/ppermute | solution.py:14
  20.6 12.8 %collective-permute-start.3 = (bf16[2,512,128]{2,1,0:T(8,128)(2,1)S(1)}, bf16[2,512,128]{2,1,0:T(8,128)(2,1)S(1)}, u32[]{:S(2)}, u32[]{:S(2)}) collective-permute-start(bf16[2,512,128]{2,1,0:T(8,128)(2,1)S(1)} %pad_maximum_fusion), channel_id=1, source_target_pairs={{0,1},{1,2},{2,3},{3,4},{4,5},{5,6},{6,7},{7,8},{8,9},{9,10},{10,1... | collective-permute-start | bytes 786440 | tf_op jit(solution)/shard_map/ppermute | solution.py:14
  34.5 5.6 %copy-start = (bf16[2560,128]{1,0:T(8,128)(2,1)}, bf16[2560,128]{1,0:T(8,128)(2,1)S(1)}, u32[]{:S(2)}) copy-start(bf16[2560,128]{1,0:T(8,128)(2,1)S(1)} %get-tuple-element.239) | copy-start | bytes 1966084 | tf_op jit(solution)/shard_map/while
  44.9 4.5 %copy-start.1 = (bf16[2560,128]{1,0:T(8,128)(2,1)S(1)}, bf16[2560,128]{1,0:T(8,128)(2,1)}, u32[]{:S(2)}) copy-start(bf16[2560,128]{1,0:T(8,128)(2,1)} %copy-done) | copy-start | bytes 1966084 | tf_op jit(solution)/shard_map/while
  55.6 5.6 %copy-start = (bf16[2560,128]{1,0:T(8,128)(2,1)}, bf16[2560,128]{1,0:T(8,128)(2,1)S(1)}, u32[]{:S(2)}) copy-start(bf16[2560,128]{1,0:T(8,128)(2,1)S(1)} %get-tuple-element.239) | copy-start | bytes 1966084 | tf_op jit(solution)/shard_map/while
  66.0 4.5 %copy-start.1 = (bf16[2560,128]{1,0:T(8,128)(2,1)S(1)}, bf16[2560,128]{1,0:T(8,128)(2,1)}, u32[]{:S(2)}) copy-start(bf16[2560,128]{1,0:T(8,128)(2,1)} %copy-done) | copy-start | bytes 1966084 | tf_op jit(solution)/shard_map/while
Sparse Core Ops, SparseCore 0:
  22.7 48.2 all-gather.1
where the time goes:
time: 120 us
  blocking collectives  29.9 us (25%)
  matrix products  22.6 us (19%)
  other arithmetic  15.2 us (13%)
  starting transfers between devices  14.9 us (12%)
  between operations  13.5 us (11%)
  waiting for transfers between devices  9.71 us (8%)
  local copies, waits for them, and re-layouts  8.13 us (7%)
  loops' own time  5.75 us (5%)
    all_to_all x1, blocking collectives, summed_on_arrival(): lax.all_to_all(parts, axis, split_axis=0, concat_axis=0, tiled=True)  29.9 us
    ppermute x4, starting transfers between devices, from_behind(): return lax.ppermute(block, axis, route)  14.9 us
    dot_general x2, matrix products, one_block(): jnp.einsum('hqk,kd->qhd', probs, value_window, preferred_element_type=jnp...  10.8 us
    ppermute x4, waiting for transfers between devices, from_behind(): return lax.ppermute(block, axis, route)  9.69 us
    reduce_sum x2, other arithmetic, one_block(): row_sum = jnp.sum(raised, axis=-1)  8.89 us
    dot_general x2, matrix products, one_block(): jnp.einsum('qhd,kd->hqk', query_part, key_window, preferred_element_type=...  6.94 us
    another operation x1, loops' own time, local(): lax.map(one_block, jnp.arange(block_count * pack_count, dtype=jnp.int32))  5.75 us
    dot_general x1, matrix products, local(): jnp.dot(attended, lax.all_gather(out_weight, 'docs', axis=1, tiled=True),...  4.89 us
  transfers between devices with their start and end apart: 5, of which 3 were waited for; matrix products, arithmetic and copies ran while one was open for 32% of the time, Pallas kernels for 0%

commit v1 on v0

v1 whole, which is shorter than its diff:
```python
import functools
import math

import jax
import jax.numpy as jnp
from jax import lax
from jax.experimental import pallas as pl
from jax.experimental.pallas import tpu as pltpu
from jax.sharding import PartitionSpec as P

MESH = pl.DeviceIdType.MESH
NT = (((1,), (1,)), ((), ()))
NN = (((1,), (0,)), ((), ()))
F32, BF16 = jnp.float32, jnp.bfloat16
BIG = float(2**20)
SCALE = 128**-0.5 * math.log2(math.e)
CK = 512
NC = 2048 // CK
NDOC = 16


def kernel(
    q_hbm, k_hbm, v_hbm, doc_ref, w_hbm, out_ref,
    qv, kb, eb, vv, vb, bias, wb, s_buf, att,
    ps2, pp, pm, po, r1p, r1m, r2p, r2m,
    lsem, kvs, kvr, wys, wyr, wzs, wzr, wss, wsr, xs, xr,
):
    h, d = lax.axis_index("heads"), lax.axis_index("docs")
    c, y, z = d % 2, (d // 2) % 4, d // 8
    chip = d // 2

    def at(zz, yy):
        return (h, (zz * 4 + yy) * 2 + c)

    sib = (h, d + 1 - 2 * c)
    nxt = (h, ((chip + 1) % 16) * 2 + c)
    prv = (h, ((chip + 15) % 16) * 2 + c)
    yp, ym = at(z, (y + 1) % 4), at(z, (y + 3) % 4)
    zp, zm = at((z + 1) % 4, y), at((z + 3) % 4, y)
    xp, xm = ((h + 1) % 4, d), ((h + 3) % 4, d)

    lq = pltpu.make_async_copy(q_hbm, qv, lsem.at[0])
    lk = pltpu.make_async_copy(k_hbm, kb.at[pl.ds(2048, 512), :], lsem.at[1])
    lv = pltpu.make_async_copy(v_hbm, vv, lsem.at[2])
    lw = pltpu.make_async_copy(w_hbm, wb.at[z, y, c], lsem.at[3])
    lv.start()
    lk.start()
    lw.start()
    lq.start()

    barrier = pltpu.get_barrier_semaphore()
    for other in (sib, nxt, prv, yp, ym, zp, zm, xp, xm):
        pl.semaphore_signal(barrier, inc=1, device_id=other, device_id_type=MESH)

    def remote(src, dst, ss, rs, dev):
        return pltpu.make_async_remote_copy(
            src_ref=src, dst_ref=dst, send_sem=ss, recv_sem=rs, device_id=dev, device_id_type=MESH
        )

    def kv(kind, part):
        src = (4, 2, 4 - 2 * c, 2 - 2 * c)[kind]
        dst = (2, 0, 3, 1)[kind]
        dev = (nxt, nxt, sib, sib)[kind]
        if part == 0:
            a = kb.at[pl.ds(pl.multiple_of(src * 512, 512), 512), :]
            b = kb.at[pl.ds(dst * 512, 512), :]
        else:
            a = vb.at[:, pl.ds(pl.multiple_of(src * 512, 512), 512)]
            b = vb.at[:, pl.ds(dst * 512, 512)]
        return remote(a, b, kvs.at[kind, part], kvr.at[kind, part], dev)

    def w_y(s):
        ref = wb.at[z, (y + s) % 4, c]
        return remote(ref, ref, wys.at[s], wyr.at[s], ym)

    def w_y_in(s):
        ref = wb.at[z, (y + s + 1) % 4, c]
        return remote(ref, ref, wys.at[s], wyr.at[s], ym)

    def w_z(s, k):
        row = (z, z, (z + 3) % 4, (z + 1) % 4)[k]
        ref = wb.at[row, (y + s) % 4, c]
        if k >= 2:
            ref = ref.at[pl.ds(32 * (k - 2), 32), :]
        return remote(ref, ref, wzs.at[s, k], wzr.at[s, k], (zp, zm, zp, zm)[k])

    def w_z_in(s, k):
        row = ((z + 3) % 4, (z + 1) % 4, (z + 2) % 4, (z + 2) % 4)[k]
        ref = wb.at[row, (y + s) % 4, c]
        if k >= 2:
            ref = ref.at[pl.ds(32 * (k - 2), 32), :]
        return remote(ref, ref, wzs.at[s, k], wzr.at[s, k], (zp, zm, zp, zm)[k])

    def w_s(k):
        ref = wb.at[(z + (0, 3, 1, 2)[k]) % 4, :, c]
        return remote(ref, ref, wss.at[k], wsr.at[k], sib)

    def w_s_in(k):
        ref = wb.at[(z + (0, 3, 1, 2)[k]) % 4, :, 1 - c]
        return remote(ref, ref, wss.at[k], wsr.at[k], sib)

    def w_step(s):
        if s > 0:
            w_y_in(s - 1).wait_recv()
        if s < 3:
            w_y(s).start()
        w_z(s, 0).start()
        w_z(s, 1).start()

    def w_forward(s):
        w_z_in(s, 0).wait_recv()
        w_z(s, 2).start()
        w_z_in(s, 1).wait_recv()
        w_z(s, 3).start()

    lv.wait()
    vb[:, 2048:] = jnp.transpose(vv[...].astype(F32)).astype(BF16)
    lk.wait()
    lw.wait()
    pl.semaphore_wait(barrier, 9)

    kv(0, 0).start()
    kv(0, 1).start()

    @pl.when(c == 0)
    def _():
        kv(2, 0).start()
        kv(2, 1).start()

    w_step(0)

    lane = lax.broadcasted_iota(jnp.int32, (128, 128), 1)
    row = lax.broadcasted_iota(jnp.int32, (128, 128), 0)
    for w in range(20):
        eb[w * 128 : (w + 1) * 128, :] = (lane == w).astype(F32).astype(BF16)
    tri = jnp.where(row <= lane, 0.0, -BIG).astype(F32)
    tri2 = jnp.concatenate([tri, tri], axis=1)
    first_block = d * 4
    block = lax.broadcasted_iota(jnp.int32, (16, 128), 1) + (first_block - 16)
    doc = jnp.zeros((16, 128), jnp.int32)
    own = [jnp.int32(0)] * 4
    end = jnp.int32(0)
    for t in range(NDOC):
        end = end + doc_ref[t]
        doc = doc + (end <= block).astype(jnp.int32)
        own = [own[i] + (end <= first_block + i).astype(jnp.int32) for i in range(4)]
    for i in range(4):
        allowed = (doc == own[i]) & (block >= 0)
        bias[i] = jnp.where(allowed, 0.0, -BIG).astype(BF16)

    for part in range(2):
        kv(0, part).wait_recv()
        kv(1, part).start()

        @pl.when(c == 0)
        def _():
            kv(3, part).start()

        @pl.when(c == 1)
        def _():
            kv(2, part).start()

        w_step(part + 1)
    w_forward(0)
    w_step(3)
    w_s(0).start()
    w_forward(1)
    for part in range(2):
        kv(1, part).wait_recv()

        @pl.when(c == 1)
        def _():
            kv(3, part).start()

    w_forward(2)
    lq.wait()
    for part in range(2):
        kv(2, part).wait_recv()
        kv(3, part).wait_recv()

    ones = jnp.ones((16, CK), BF16)

    def scores(i, hp, slot, ck, mx):
        k0 = pl.multiple_of((i + 1) * 128 + ck * CK, 128)
        q2 = qv[pl.ds(pl.multiple_of(i * 128, 128), 128), hp * 256 : hp * 256 + 256]
        b = jnp.concatenate([bias[i]] * 8, axis=0)
        qq = jnp.concatenate(
            [
                jnp.concatenate([q2[:, :128], b], axis=1),
                jnp.concatenate([q2[:, 128:], b], axis=1),
            ],
            axis=0,
        )
        kk = jnp.concatenate([kb[pl.ds(k0, CK), :], eb[pl.ds(k0, CK), :]], axis=1)
        s = lax.dot_general(kk, qq, NT, preferred_element_type=F32)
        if ck == NC - 1:
            s = jnp.concatenate([s[: CK - 128], s[CK - 128 :] + tri2], axis=0)
        s_buf[slot, ck * CK : (ck + 1) * CK, :] = s
        n = jnp.max(s.reshape(CK // 8, 8, 256), axis=0)
        return n if mx is None else jnp.maximum(mx, n)

    def weigh(i, slot, ck, m, acc):
        k0 = pl.multiple_of((i + 1) * 128 + ck * CK, 128)
        s = s_buf[slot, ck * CK : (ck + 1) * CK, :]
        p = jnp.exp2((s - m) * SCALE).astype(BF16)
        lhs = jnp.concatenate([vb[:, pl.ds(k0, CK)], ones], axis=0)
        t = lax.dot_general(lhs, p, NN, preferred_element_type=F32)
        return t if acc is None else acc + t

    def top(mx):
        return jnp.max(mx, axis=0, keepdims=True)

    def project(j):
        w = wb[j].reshape(512, 1024)
        return lax.dot_general(w, att[...], NN, preferred_element_type=F32)

    lo, hi = pl.ds(0, 256), pl.ds(256, 256)

    def x_copy(i, k):
        src, dst = (
            (ps2.at[i, lo], r1p.at[i]),
            (ps2.at[i, hi], r1m.at[i]),
            (pp.at[i, hi], r2p.at[i, hi]),
            (pm.at[i, lo], r2m.at[i, lo]),
            (pp.at[i, lo], r2p.at[i, lo]),
            (pm.at[i, hi], r2m.at[i, hi]),
        )[k]
        return remote(src, dst, xs.at[i, k], xr.at[i, k], (xp, xm)[k % 2])

    def merge(i):
        x_copy(i, 0).wait_recv()
        pp[i, lo, :] = (pp[i, lo, :].astype(F32) + r1p[i].astype(F32)).astype(BF16)
        x_copy(i, 4).start()
        x_copy(i, 1).wait_recv()
        pm[i, hi, :] = (pm[i, hi, :].astype(F32) + r1m[i].astype(F32)).astype(BF16)
        x_copy(i, 5).start()

    mx = None
    for ck in range(NC):
        mx = scores(0, 0, 0, ck, mx)

    def one(i, m):
        for u in range(4):
            slot = u % 2
            ni, nu = (i, u + 1) if u < 3 else (jnp.minimum(i + 1, 3), 0)
            mx, acc = None, None
            for ck in range(NC):
                mx = scores(ni, nu, 1 - slot, ck, mx)
                acc = weigh(i, slot, ck, m, acc)
            m = top(mx)
            o = (acc[:128] / acc[128:129]).astype(BF16)
            att[u * 256 : u * 256 + 128, :] = o[:, :128]
            att[u * 256 + 128 : u * 256 + 256, :] = o[:, 128:]

        @pl.when(i == 0)
        def _():
            w_forward(3)
            w_s(1).start()
            w_s(2).start()
            for s in range(4):
                w_z_in(s, 2).wait_recv()
                w_z_in(s, 3).wait_recv()
            w_s(3).start()
            for k in range(4):
                w_s_in(k).wait_recv()

        ps2[i] = project((h + 2) % 4).astype(BF16)
        x_copy(i, 0).start()
        x_copy(i, 1).start()
        pp[i] = project((h + 1) % 4).astype(BF16)
        x_copy(i, 2).start()
        pm[i] = project((h + 3) % 4).astype(BF16)
        x_copy(i, 3).start()

        @pl.when(i > 0)
        def _():
            merge(i - 1)

        po[i] = project(h)
        return m

    lax.fori_loop(0, 4, one, top(mx))
    merge(3)

    def finish(i, _):
        for k in range(2, 6):
            x_copy(i, k).wait_recv()
        total = po[i] + r2p[i].astype(F32) + r2m[i].astype(F32)
        out_ref[pl.ds(pl.multiple_of(i * 128, 128), 128), :] = jnp.transpose(total).astype(BF16)
        for k in range(6):
            x_copy(i, k).wait_send()
        return 0

    lax.fori_loop(0, 4, finish, 0)
    for kind in range(4):
        for part in range(2):
            kv(kind, part).wait_send()
    for s in range(4):
        if s < 3:
            w_y(s).wait_send()
        for k in range(4):
            w_z(s, k).wait_send()
        w_s(s).wait_send()


def local(query_rows, key_rows, value_rows, doc_blocks, out_weight):
    hbm = pl.BlockSpec(memory_space=pl.ANY)
    dma = pltpu.SemaphoreType.DMA
    return pl.pallas_call(
        kernel,
        out_shape=jax.ShapeDtypeStruct((512, 512), BF16),
        in_specs=[hbm, hbm, hbm, pl.BlockSpec(memory_space=pltpu.SMEM), hbm],
        out_specs=pl.BlockSpec(memory_space=pltpu.VMEM),
        scratch_shapes=[
            pltpu.VMEM((512, 1024), BF16),
            pltpu.VMEM((2560, 128), BF16),
            pltpu.VMEM((2560, 128), BF16),
            pltpu.VMEM((512, 128), BF16),
            pltpu.VMEM((128, 2560), BF16),
            pltpu.VMEM((4, 16, 128), BF16),
            pltpu.VMEM((4, 4, 2, 64, 1024), BF16),
            pltpu.VMEM((2, 2048, 256), F32),
            pltpu.VMEM((1024, 128), BF16),
            pltpu.VMEM((4, 512, 128), BF16),
            pltpu.VMEM((4, 512, 128), BF16),
            pltpu.VMEM((4, 512, 128), BF16),
            pltpu.VMEM((4, 512, 128), F32),
            pltpu.VMEM((4, 256, 128), BF16),
            pltpu.VMEM((4, 256, 128), BF16),
            pltpu.VMEM((4, 512, 128), BF16),
            pltpu.VMEM((4, 512, 128), BF16),
            dma((4,)),
            dma((4, 2)), dma((4, 2)),
            dma((3,)), dma((3,)),
            dma((4, 4)), dma((4, 4)),
            dma((4,)), dma((4,)),
            dma((4, 6)), dma((4, 6)),
        ],
        compiler_params=pltpu.CompilerParams(
            collective_id=0, has_side_effects=True, vmem_limit_bytes=48 * 2**20
        ),
    )(query_rows, key_rows, value_rows, doc_blocks, out_weight.T)


def solution(mesh):
    placed = (P("docs", "heads"), P("docs", "heads"), P("docs", "heads"), P(), P("heads", "docs"))
    return jax.shard_map(
        local, mesh=mesh, in_specs=placed, out_specs=P("docs", "heads"), check_vma=False
    )
```

time: 120 us -> 71 us (0.59)
  Pallas kernels: 0 us -> 65.4 us
  blocking collectives: 29.9 us -> 0 us
  matrix products: 22.6 us -> 0 us
  other arithmetic: 15.2 us -> 0 us
  starting transfers between devices: 14.9 us -> 0 us
  between operations: 13.5 us -> 0.01 us
  waiting for transfers between devices: 9.71 us -> 0 us
  loops' own time: 5.75 us -> 0 us
  local copies, waits for them, and re-layouts: 8.13 us -> 5.39 us
    pallas_call x0 -> x1, Pallas kernels: none -> 65.4 us  [local(): pl.pallas_call(kernel, out_shape=jax.ShapeDtypeStruct((512, 512), BF16),...]
    all_to_all x1 -> x0, blocking collectives: 29.9 us -> none  [summed_on_arrival(): lax.all_to_all(parts, axis, split_axis=0, concat_axis=0, tiled=True)]
    dot_general x5 -> x0, matrix products: 22.6 us -> none  [the longest x2 10.8 us: one_block(): jnp.einsum('hqk,kd->qhd', probs, value_window, preferred_element_type=jnp...]
    ppermute x4 -> x0, starting transfers between devices: 14.9 us -> none  [from_behind(): return lax.ppermute(block, axis, route)]
    reduce_sum x4 -> x0, other arithmetic: 10.2 us -> none  [the longest x2 8.89 us: one_block(): row_sum = jnp.sum(raised, axis=-1)]
    ppermute x4 -> x0, waiting for transfers between devices: 9.69 us -> none  [from_behind(): return lax.ppermute(block, axis, route)]
    another operation x1 -> x0, loops' own time: 5.75 us -> none  [local(): lax.map(one_block, jnp.arange(block_count * pack_count, dtype=jnp.int32))]
    unnamed x4 -> x11, local copies, waits for them, and re-layouts: 0.12 us -> 5.39 us
  transfers between devices with their start and end apart: 5 -> 0, of which waited for: 3 -> 0; matrix products, arithmetic and copies ran while one was open for 32% -> 0% of each run, Pallas kernels for 0% -> 0%
where the time goes in v1:
time: 71 us; the launch traced here: 70.8 us
  Pallas kernels  65.4 us (92%)
  local copies, waits for them, and re-layouts  5.39 us (8%)
    pallas_call x1, Pallas kernels, local(): pl.pallas_call(kernel, out_shape=jax.ShapeDtypeStruct((512, 512), BF16),...  65.4 us
    unnamed x11, local copies, waits for them, and re-layouts  5.39 us

profile of v1, /device:TPU:1, one launch (start us, length us, event | category | flops | bytes accessed | tf_op | source)
XLA Modules:
  0.0 70.8 jit_solution(13865955272603894205)
XLA Ops:
  0.0 0.0 copy-start.4
  0.0 0.7 copy-done.4
  0.7 0.0 copy-start
  0.7 1.2 %copy-done = bf16[512,1024]{1,0:T(8,128)(2,1)S(1)} copy-done((bf16[512,1024]{1,0:T(8,128)(2,1)S(1)}, bf16[512,1024]{1,0:T(8,128)(2,1)}, u32[]{:S(2)}) %copy-start) | copy-done | bytes 1048600
  1.9 0.0 copy-start.1
  1.9 0.9 %copy-done.1 = bf16[512,128]{1,0:T(8,128)(2,1)S(1)} copy-done((bf16[512,128]{1,0:T(8,128)(2,1)S(1)}, bf16[512,128]{1,0:T(8,128)(2,1)}, u32[]{:S(2)}) %copy-start.1) | copy-done | bytes 131096
  2.8 0.0 copy-start.2
  2.8 0.9 %copy-done.2 = bf16[512,128]{1,0:T(8,128)(2,1)S(1)} copy-done((bf16[512,128]{1,0:T(8,128)(2,1)S(1)}, bf16[512,128]{1,0:T(8,128)(2,1)}, u32[]{:S(2)}) %copy-start.2) | copy-done | bytes 131096
  3.7 0.0 copy-start.3
  3.7 0.9 %copy-done.3 = bf16[1024,64]{0,1:T(8,128)(2,1)S(1)} copy-done((bf16[1024,64]{0,1:T(8,128)(2,1)S(1)}, bf16[1024,64]{0,1:T(8,128)(2,1)}, u32[]{:S(2)}) %copy-start.3) | copy-done | bytes 131096
  4.6 65.4 %shard_map.55 = bf16[512,512]{1,0:T(8,128)(2,1)S(1)} custom-call(bf16[512,1024]{1,0:T(8,128)(2,1)S(1)} %copy-done, bf16[512,128]{1,0:T(8,128)(2,1)S(1)} %copy-done.1, bf16[512,128]{1,0:T(8,128)(2,1)S(1)} %copy-done.2, s32[16]{0:T(128)S(1)} %copy-done.4, bf16[64,1024]{1,0:T(8,128)(2,1)S(1)} %bitcast.1), custom_call_target="tpu_custom_call" | custom-call | tf_op jit(solution)/shard_map/pallas_call | solution.py:309
  70.0 0.8 %copy.7 = bf16[512,512]{1,0:T(8,128)(2,1)} copy(bf16[512,512]{1,0:T(8,128)(2,1)S(1)} %shard_map.55) | data formatting | bytes 1048576
Async XLA Ops:
  0.0 0.7 copy-start.4
  0.7 1.2 %copy-start = (bf16[512,1024]{1,0:T(8,128)(2,1)S(1)}, bf16[512,1024]{1,0:T(8,128)(2,1)}, u32[]{:S(2)}) copy-start(bf16[512,1024]{1,0:T(8,128)(2,1)} %q_hbm.1) | copy-start | bytes 3145732
  1.9 0.9 %copy-start.1 = (bf16[512,128]{1,0:T(8,128)(2,1)S(1)}, bf16[512,128]{1,0:T(8,128)(2,1)}, u32[]{:S(2)}) copy-start(bf16[512,128]{1,0:T(8,128)(2,1)} %k_hbm.1) | copy-start | bytes 393220
  2.8 0.9 %copy-start.2 = (bf16[512,128]{1,0:T(8,128)(2,1)S(1)}, bf16[512,128]{1,0:T(8,128)(2,1)}, u32[]{:S(2)}) copy-start(bf16[512,128]{1,0:T(8,128)(2,1)} %v_hbm.1) | copy-start | bytes 393220
  3.7 0.9 %copy-start.3 = (bf16[1024,64]{0,1:T(8,128)(2,1)S(1)}, bf16[1024,64]{0,1:T(8,128)(2,1)}, u32[]{:S(2)}) copy-start(bf16[1024,64]{0,1:T(8,128)(2,1)} %param.9) | copy-start | bytes 393220

commit v2 on v1

v2 whole, which is shorter than its diff:
```python
import functools
import math

import jax
import jax.numpy as jnp
from jax import lax
from jax.experimental import pallas as pl
from jax.experimental.pallas import tpu as pltpu
from jax.sharding import PartitionSpec as P

MESH = pl.DeviceIdType.MESH
NT = (((1,), (1,)), ((), ()))
NN = (((1,), (0,)), ((), ()))
F32, BF16 = jnp.float32, jnp.bfloat16
BIG = float(2**20)
SCALE = 128**-0.5 * math.log2(math.e)
CK = 512
NDOC = 16


def chunks(total):
    return [(o, min(CK, total - o)) for o in range(0, total, CK)]


def kernel(
    q_hbm, k_hbm, v_hbm, doc_ref, w_hbm, out_hbm,
    qv, kb, eb, vv, vb, bias, wb, s_buf, m_buf, a_buf, att,
    ps2, pp, pm, po, r1p, r1m, r2p, r2m, obuf,
    lsem, kvs, kvr, ws, wr, xs, xr,
):
    h, d = lax.axis_index("heads"), lax.axis_index("docs")
    c, y, z = d % 2, (d // 2) % 4, d // 8
    chip = d // 2

    def at(zz, yy):
        return (h, ((zz % 4) * 4 + yy % 4) * 2 + c)

    sib = (h, d + 1 - 2 * c)
    nxt = (h, ((chip + 1) % 16) * 2 + c)
    prv = (h, ((chip + 15) % 16) * 2 + c)
    yp, ym = at(z, y + 1), at(z, y + 3)
    zp, zm = at(z + 1, y), at(z + 3, y)
    xp, xm = ((h + 1) % 4, d), ((h + 3) % 4, d)

    lq = pltpu.make_async_copy(q_hbm, qv, lsem.at[0])
    lk = pltpu.make_async_copy(k_hbm, kb.at[pl.ds(2048, 512), :], lsem.at[1])
    lv = pltpu.make_async_copy(v_hbm, vv, lsem.at[2])
    lw = pltpu.make_async_copy(w_hbm, wb.at[z, y, c], lsem.at[3])
    lv.start()
    lk.start()
    lw.start()
    lq.start()

    barrier = pltpu.get_barrier_semaphore()
    for other in (sib, nxt, prv, yp, ym, zp, zm, xp, xm):
        pl.semaphore_signal(barrier, inc=1, device_id=other, device_id_type=MESH)

    def remote(src, dst, ss, rs, dev):
        return pltpu.make_async_remote_copy(
            src_ref=src, dst_ref=dst, send_sem=ss, recv_sem=rs, device_id=dev, device_id_type=MESH
        )

    def kv(kind, part):
        src = (4, 2, 4 - 2 * c, 2 - 2 * c)[kind]
        dst = (2, 0, 3, 1)[kind]
        dev = (nxt, nxt, sib, sib)[kind]
        if part == 0:
            a = kb.at[pl.ds(pl.multiple_of(src * 512, 512), 512), :]
            b = kb.at[pl.ds(dst * 512, 512), :]
        else:
            a = vb.at[:, pl.ds(pl.multiple_of(src * 512, 512), 512)]
            b = vb.at[:, pl.ds(dst * 512, 512)]
        return remote(a, b, kvs.at[kind, part], kvr.at[kind, part], dev)

    def w_ref(half, a, b):
        zz, yy = (z + b, y + a) if half == 0 else (z + a, y + b)
        return wb.at[zz % 4, yy % 4, c, pl.ds(32 * half, 32), :]

    def w_row(half, b, core):
        if half == 0:
            return wb.at[(z + b) % 4, :, core, pl.ds(0, 32), :]
        return wb.at[:, (y + b) % 4, core, pl.ds(32, 32), :]

    RING, OWN, FWD, PLUS, SHARE = range(5)

    def w_send(kind, half, s):
        if kind == SHARE:
            ref, dev = w_row(half, s, c), sib
        else:
            ref = w_ref(half, s, 1 if kind == FWD else 0)
            first, second, plus = (ym, zm, zp) if half == 0 else (zm, ym, yp)
            dev = (first, second, second, plus)[kind]
        return remote(ref, ref, ws.at[kind, half, s], wr.at[kind, half, s], dev)

    def w_come(kind, half, s):
        if kind == SHARE:
            ref = w_row(half, s, 1 - c)
        else:
            ref = w_ref(half, s + 1 if kind == RING else s, (0, 1, 2, 3)[kind])
        return remote(ref, ref, ws.at[kind, half, s], wr.at[kind, half, s], sib)

    def w_ring(s):
        for half in range(2):
            if s > 0:
                w_come(RING, half, s - 1).wait_recv()
            if s < 3:
                w_send(RING, half, s).start()
        for half in range(2):
            w_send(OWN, half, s).start()

    def w_fwd(s):
        for half in range(2):
            w_come(OWN, half, s).wait_recv()
            w_send(FWD, half, s).start()

    def w_share(b):
        for half in range(2):
            w_send(SHARE, half, b).start()

    lv.wait()
    vb[:, 2048:] = jnp.transpose(vv[...].astype(F32)).astype(BF16)

    lane = lax.broadcasted_iota(jnp.int32, (128, 128), 1)
    row = lax.broadcasted_iota(jnp.int32, (128, 128), 0)
    for w in range(20):
        eb[w * 128 : (w + 1) * 128, :] = (lane == w).astype(F32).astype(BF16)
    tri = jnp.where(row <= lane, 0.0, -BIG).astype(F32)
    tri2 = jnp.concatenate([tri, tri], axis=1)
    first_block = d * 4
    block = lax.broadcasted_iota(jnp.int32, (16, 128), 1) + (first_block - 16)
    doc = jnp.zeros((16, 128), jnp.int32)
    own = [jnp.int32(0)] * 4
    end = jnp.int32(0)
    for t in range(NDOC):
        end = end + doc_ref[t]
        doc = doc + (end <= block).astype(jnp.int32)
        own = [own[i] + (end <= first_block + i).astype(jnp.int32) for i in range(4)]
    for i in range(4):
        allowed = (doc == own[i]) & (block >= 0)
        bias[i] = jnp.where(allowed, 0.0, -BIG).astype(BF16)

    lk.wait()
    lw.wait()
    pl.semaphore_wait(barrier, 9)

    kv(0, 0).start()
    kv(0, 1).start()

    @pl.when(c == 0)
    def _():
        kv(2, 0).start()
        kv(2, 1).start()

    w_ring(0)
    lq.wait()

    def kv_near(part):
        kv(0, part).wait_recv()
        kv(1, part).start()

        @pl.when(c == 0)
        def _():
            kv(3, part).start()

        @pl.when(c == 1)
        def _():
            kv(2, part).start()

    def kv_far(part):
        kv(1, part).wait_recv()

        @pl.when(c == 1)
        def _():
            kv(3, part).start()

    w_ring(1)
    kv_near(0)
    w_fwd(0)
    kv_near(1)
    w_ring(2)
    kv(2, 0).wait_recv()
    kv(2, 1).wait_recv()

    def span(phase, i):
        return (1024, (9 + i) * 128) if phase == 0 else ((i + 1) * 128, (7 - i) * 128)

    def scores(phase, hp, i, slot, ck, mx):
        base, total = span(phase, i)
        o, n = chunks(total)[ck]
        q2 = qv[i * 128 : i * 128 + 128, pl.ds(pl.multiple_of(hp * 256, 256), 256)]
        b = jnp.concatenate([bias[i]] * 8, axis=0)
        qq = jnp.concatenate(
            [
                jnp.concatenate([q2[:, :128], b], axis=1),
                jnp.concatenate([q2[:, 128:], b], axis=1),
            ],
            axis=0,
        )
        rows = slice(base + o, base + o + n)
        kk = jnp.concatenate([kb[rows, :], eb[rows, :]], axis=1)
        s = lax.dot_general(kk, qq, NT, preferred_element_type=F32)
        if phase == 0 and o + n == total:
            last = s[n - 128 :] + tri2
            s = last if n == 128 else jnp.concatenate([s[: n - 128], last], axis=0)
        s_buf[slot, o : o + n, :] = s
        new = jnp.max(s.reshape(n // 8, 8, 256), axis=0)
        return new if mx is None else jnp.maximum(mx, new)

    def weigh(phase, i, slot, ck, m, acc):
        base, total = span(phase, i)
        o, n = chunks(total)[ck]
        s = s_buf[slot, o : o + n, :]
        p = jnp.exp2((s - m) * SCALE).astype(BF16)
        lhs = jnp.concatenate([vb[:, base + o : base + o + n], jnp.ones((16, n), BF16)], axis=0)
        t = lax.dot_general(lhs, p, NN, preferred_element_type=F32)
        return t if acc is None else acc + t

    def attention(phase, between):
        def top(hp, i, mx):
            m = jnp.max(mx, axis=0, keepdims=True)
            return m if phase == 0 else jnp.maximum(m, m_buf[hp, i, 0:1, :])

        def one(hp, m):
            for i in range(4):
                slot = i % 2
                nhp, ni = (hp, i + 1) if i < 3 else (jnp.minimum(hp + 1, 3), 0)
                mx, acc = None, None
                na, nb = len(chunks(span(phase, ni)[1])), len(chunks(span(phase, i)[1]))
                for ck in range(max(na, nb)):
                    if ck < na:
                        mx = scores(phase, nhp, ni, 1 - slot, ck, mx)
                    if ck < nb:
                        acc = weigh(phase, i, slot, ck, m, acc)
                if phase == 0:
                    m_buf[hp, i] = jnp.broadcast_to(m, (8, 256))
                    a_buf[hp, i] = acc[:136]
                else:
                    alpha = jnp.exp2((m_buf[hp, i, 0:1, :] - m) * SCALE)
                    acc = acc[:136] + a_buf[hp, i] * alpha
                    out = (acc[:128] / acc[128:129]).astype(BF16)
                    f = pl.multiple_of(hp * 256, 256)
                    att[pl.ds(f, 128), i * 128 : i * 128 + 128] = out[:, :128]
                    att[pl.ds(f + 128, 128), i * 128 : i * 128 + 128] = out[:, 128:]
                m = top(nhp, ni, mx)
            between(hp)
            return m

        mx = None
        for ck in range(len(chunks(span(phase, 0)[1]))):
            mx = scores(phase, 0, 0, 0, ck, mx)
        lax.fori_loop(0, 4, one, top(0, 0, mx))

    def first(hp):
        @pl.when(hp == 0)
        def _():
            w_fwd(1)

        @pl.when(hp == 1)
        def _():
            kv_far(0)
            w_ring(3)

        @pl.when(hp == 2)
        def _():
            w_share(0)
            w_fwd(2)

    attention(0, first)
    kv_far(1)
    for half in range(2):
        for s in range(4):
            w_send(PLUS, half, s).start()
    w_fwd(3)
    w_share(1)
    for part in range(2):
        kv(3, part).wait_recv()
    attention(1, lambda hp: None)

    for b in (2, 3):
        for half in range(2):
            for s in range(4):
                w_come((RING, OWN, FWD, PLUS)[b], half, s).wait_recv()
        w_share(b)
    for b in range(4):
        for half in range(2):
            w_come(SHARE, half, b).wait_recv()

    lo, hi = pl.ds(0, 256), pl.ds(256, 256)

    def x_copy(i, k):
        src, dst = (
            (ps2.at[i, lo], r1p.at[i]),
            (ps2.at[i, hi], r1m.at[i]),
            (pp.at[i, hi], r2p.at[i, hi]),
            (pm.at[i, lo], r2m.at[i, lo]),
            (pp.at[i, lo], r2p.at[i, lo]),
            (pm.at[i, hi], r2m.at[i, hi]),
        )[k]
        return remote(src, dst, xs.at[i, k], xr.at[i, k], (xp, xm)[k % 2])

    def project(j, into, kinds):
        w = wb[j].reshape(512, 1024)
        for pair in range(2):
            t = lax.dot_general(w, att[:, pair * 256 : pair * 256 + 256], NN, preferred_element_type=F32).astype(BF16)
            for u in range(2):
                into[2 * pair + u] = t[:, u * 128 : u * 128 + 128]
                for k in kinds:
                    x_copy(2 * pair + u, k).start()

    project((h + 2) % 4, ps2, (0, 1))
    project((h + 1) % 4, pp, (2,))
    project((h + 3) % 4, pm, (3,))
    project(h, po, ())

    def merge(i, _):
        x_copy(i, 0).wait_recv()
        pp[i, lo, :] = (pp[i, lo, :].astype(F32) + r1p[i].astype(F32)).astype(BF16)
        x_copy(i, 4).start()
        x_copy(i, 1).wait_recv()
        pm[i, hi, :] = (pm[i, hi, :].astype(F32) + r1m[i].astype(F32)).astype(BF16)
        x_copy(i, 5).start()
        return 0

    lax.fori_loop(0, 4, merge, 0)

    def write(i):
        return pltpu.make_async_copy(
            obuf.at[i], out_hbm.at[pl.ds(pl.multiple_of(i * 128, 128), 128), :], lsem.at[4 + i]
        )

    def finish(i, _):
        for k in range(2, 6):
            x_copy(i, k).wait_recv()
        total = po[i].astype(F32) + r2p[i].astype(F32) + r2m[i].astype(F32)
        obuf[i] = jnp.transpose(total).astype(BF16)
        write(i).start()
        for k in range(6):
            x_copy(i, k).wait_send()
        return 0

    lax.fori_loop(0, 4, finish, 0)
    for i in range(4):
        write(i).wait()
    for kind in range(4):
        for part in range(2):
            kv(kind, part).wait_send()
    for half in range(2):
        for kind in range(5):
            for s in range(3 if kind == RING else 4):
                w_send(kind, half, s).wait_send()


def local(query_rows, key_rows, value_rows, doc_blocks, out_weight):
    hbm = pl.BlockSpec(memory_space=pl.ANY)
    dma = pltpu.SemaphoreType.DMA
    return pl.pallas_call(
        kernel,
        out_shape=jax.ShapeDtypeStruct((512, 512), BF16),
        in_specs=[hbm, hbm, hbm, pl.BlockSpec(memory_space=pltpu.SMEM), hbm],
        out_specs=hbm,
        scratch_shapes=[
            pltpu.VMEM((512, 1024), BF16),
            pltpu.VMEM((2560, 128), BF16),
            pltpu.VMEM((2560, 128), BF16),
            pltpu.VMEM((512, 128), BF16),
            pltpu.VMEM((128, 2560), BF16),
            pltpu.VMEM((4, 16, 128), BF16),
            pltpu.VMEM((4, 4, 2, 64, 1024), BF16),
            pltpu.VMEM((2, 1536, 256), F32),
            pltpu.VMEM((4, 4, 8, 256), F32),
            pltpu.VMEM((4, 4, 136, 256), F32),
            pltpu.VMEM((1024, 512), BF16),
            pltpu.VMEM((4, 512, 128), BF16),
            pltpu.VMEM((4, 512, 128), BF16),
            pltpu.VMEM((4, 512, 128), BF16),
            pltpu.VMEM((4, 512, 128), BF16),
            pltpu.VMEM((4, 256, 128), BF16),
            pltpu.VMEM((4, 256, 128), BF16),
            pltpu.VMEM((4, 512, 128), BF16),
            pltpu.VMEM((4, 512, 128), BF16),
            pltpu.VMEM((4, 128, 512), BF16),
            dma((8,)),
            dma((4, 2)), dma((4, 2)),
            dma((5, 2, 4)), dma((5, 2, 4)),
            dma((4, 6)), dma((4, 6)),
        ],
        compiler_params=pltpu.CompilerParams(
            collective_id=0, has_side_effects=True, vmem_limit_bytes=62 * 2**20
        ),
    )(query_rows, key_rows, value_rows, doc_blocks, out_weight.T)


def solution(mesh):
    placed = (P("docs", "heads"), P("docs", "heads"), P("docs", "heads"), P(), P("heads", "docs"))
    return jax.shard_map(
        local, mesh=mesh, in_specs=placed, out_specs=P("docs", "heads"), check_vma=False
    )
```

time: 71 us -> 55.5 us (0.78)
  Pallas kernels: 65.4 us -> 53.5 us
  local copies, waits for them, and re-layouts: 5.39 us -> 1.87 us
    pallas_call x1, Pallas kernels: 65.4 us -> 53.5 us  [local(): pl.pallas_call(kernel, out_shape=jax.ShapeDtypeStruct((512, 512), BF16),...]
    unnamed x11 -> x1, local copies, waits for them, and re-layouts: 5.39 us -> 1.87 us
where the time goes in v2:
time: 55.5 us; the launch traced here: 55.3 us
  Pallas kernels  53.5 us (96%)
  local copies, waits for them, and re-layouts  1.87 us (3%)
    pallas_call x1, Pallas kernels, local(): pl.pallas_call(kernel, out_shape=jax.ShapeDtypeStruct((512, 512), BF16),...  53.5 us
    unnamed x1, local copies, waits for them, and re-layouts  1.87 us

profile of v2, /device:TPU:1, one launch (start us, length us, event | category | flops | bytes accessed | tf_op | source)
XLA Modules:
  0.0 55.3 jit_solution(14883546249530652917)
XLA Ops:
  0.0 53.5 %shard_map.55 = bf16[512,512]{1,0:T(8,128)(2,1)} custom-call(bf16[512,1024]{1,0:T(8,128)(2,1)} %q_hbm.1, bf16[512,128]{1,0:T(8,128)(2,1)} %k_hbm.1, bf16[512,128]{1,0:T(8,128)(2,1)} %v_hbm.1, s32[16]{0:T(128)} %doc_ref.1, bf16[64,1024]{1,0:T(8,128)(2,1)} %bitcast.1), custom_call_target="tpu_custom_call" | custom-call | tf_op jit(solution)/shard_map/pallas_call | solution.py:356
  53.5 1.9 %copy.7 = bf16[512,512]{1,0:T(8,128)(2,1)} copy(bf16[512,512]{1,0:T(8,128)(2,1)} %shard_map.55) | data formatting | bytes 1048576

commit v3 on v2

--- a/solution.py
+++ b/solution.py
@@ -25,7 +25,7 @@
 def kernel(
     q_hbm, k_hbm, v_hbm, doc_ref, w_hbm, out_hbm,
     qv, kb, eb, vv, vb, bias, wb, s_buf, m_buf, a_buf, att,
-    ps2, pp, pm, po, r1p, r1m, r2p, r2m, obuf,
+    pb, r1p, r1m, r2p, r2m, obuf,
     lsem, kvs, kvr, ws, wr, xs, xr,
 ):
     h, d = lax.axis_index("heads"), lax.axis_index("docs")
@@ -72,50 +72,48 @@
             b = vb.at[:, pl.ds(dst * 512, 512)]
         return remote(a, b, kvs.at[kind, part], kvr.at[kind, part], dev)
 
-    def w_ref(half, a, b):
-        zz, yy = (z + b, y + a) if half == 0 else (z + a, y + b)
-        return wb.at[zz % 4, yy % 4, c, pl.ds(32 * half, 32), :]
-
-    def w_row(half, b, core):
-        if half == 0:
-            return wb.at[(z + b) % 4, :, core, pl.ds(0, 32), :]
-        return wb.at[:, (y + b) % 4, core, pl.ds(32, 32), :]
-
-    RING, OWN, FWD, PLUS, SHARE = range(5)
-
-    def w_send(kind, half, s):
-        if kind == SHARE:
-            ref, dev = w_row(half, s, c), sib
+    def w_ref(a, b, core):
+        return wb.at[(z + a) % 4, (y + b) % 4, core]
+
+    RING, OWN, FWD, PLUS, SHARE = 0, 1, 2, 3, 4
+
+    def w_send(kind, s):
+        if kind == RING:
+            ref, dev = w_ref(s, 0, c), zm
+        elif kind >= SHARE:
+            ref, dev = w_ref(s, kind - SHARE, c), sib
+        elif kind == OWN or s == 0 or (kind == PLUS and s == 2):
+            ref = w_ref(s, 1 if kind == FWD else 0, c)
+            dev = yp if kind == PLUS else ym
         else:
-            ref = w_ref(half, s, 1 if kind == FWD else 0)
-            first, second, plus = (ym, zm, zp) if half == 0 else (zm, ym, yp)
-            dev = (first, second, second, plus)[kind]
-        return remote(ref, ref, ws.at[kind, half, s], wr.at[kind, half, s], dev)
-
-    def w_come(kind, half, s):
-        if kind == SHARE:
-            ref = w_row(half, s, 1 - c)
+            ref = w_ref(1 if s == 2 else 0, kind, c)
+            dev = zp if s == 3 else zm
+        return remote(ref, ref, ws.at[kind, s], wr.at[kind, s], dev)
+
+    def w_come(kind, s):
+        if kind == RING:
+            ref = w_ref(s + 1, 0, c)
+        elif kind >= SHARE:
+            ref = w_ref(s, kind - SHARE, 1 - c)
         else:
-            ref = w_ref(half, s + 1 if kind == RING else s, (0, 1, 2, 3)[kind])
-        return remote(ref, ref, ws.at[kind, half, s], wr.at[kind, half, s], sib)
+            ref = w_ref(s, (0, 1, 2, 3)[kind], c)
+        return remote(ref, ref, ws.at[kind, s], wr.at[kind, s], sib)
+
+    def w_own(s):
+        w_send(OWN, s).start()
+        w_send(SHARE, s).start()
+
+    def w_fwd(s):
+        w_come(OWN, s).wait_recv()
+        if s == 0:
+            w_send(FWD, 0).start()
+        w_send(SHARE + 1, s).start()
 
     def w_ring(s):
-        for half in range(2):
-            if s > 0:
-                w_come(RING, half, s - 1).wait_recv()
-            if s < 3:
-                w_send(RING, half, s).start()
-        for half in range(2):
-            w_send(OWN, half, s).start()
-
-    def w_fwd(s):
-        for half in range(2):
-            w_come(OWN, half, s).wait_recv()
-            w_send(FWD, half, s).start()
-
-    def w_share(b):
-        for half in range(2):
-            w_send(SHARE, half, b).start()
+        w_come(RING, s - 1).wait_recv()
+        if s < 3:
+            w_send(RING, s).start()
+        w_own(s)
 
     lv.wait()
     vb[:, 2048:] = jnp.transpose(vv[...].astype(F32)).astype(BF16)
@@ -151,7 +149,8 @@
         kv(2, 0).start()
         kv(2, 1).start()
 
-    w_ring(0)
+    w_send(RING, 0).start()
+    w_own(0)
     lq.wait()
 
     def kv_near(part):
@@ -173,16 +172,8 @@
         def _():
             kv(3, part).start()
 
-    w_ring(1)
-    kv_near(0)
-    w_fwd(0)
-    kv_near(1)
-    w_ring(2)
-    kv(2, 0).wait_recv()
-    kv(2, 1).wait_recv()
-
     def span(phase, i):
-        return (1024, (9 + i) * 128) if phase == 0 else ((i + 1) * 128, (7 - i) * 128)
+        return ((2048, (i + 1) * 128), (1024, 1024), ((i + 1) * 128, (7 - i) * 128))[phase]
 
     def scores(phase, hp, i, slot, ck, mx):
         base, total = span(phase, i)
@@ -231,12 +222,14 @@
                         mx = scores(phase, nhp, ni, 1 - slot, ck, mx)
                     if ck < nb:
                         acc = weigh(phase, i, slot, ck, m, acc)
-                if phase == 0:
+                acc = acc[:136]
+                if phase > 0:
+                    alpha = jnp.exp2((m_buf[hp, i, 0:1, :] - m) * SCALE)
+                    acc = acc + a_buf[hp, i] * alpha
+                if phase < 2:
                     m_buf[hp, i] = jnp.broadcast_to(m, (8, 256))
-                    a_buf[hp, i] = acc[:136]
+                    a_buf[hp, i] = acc
                 else:
-                    alpha = jnp.exp2((m_buf[hp, i, 0:1, :] - m) * SCALE)
-                    acc = acc[:136] + a_buf[hp, i] * alpha
                     out = (acc[:128] / acc[128:129]).astype(BF16)
                     f = pl.multiple_of(hp * 256, 256)
                     att[pl.ds(f, 128), i * 128 : i * 128 + 128] = out[:, :128]
@@ -250,6 +243,15 @@
             mx = scores(phase, 0, 0, 0, ck, mx)
         lax.fori_loop(0, 4, one, top(0, 0, mx))
 
+    attention(0, lambda hp: None)
+    w_ring(1)
+    kv_near(0)
+    kv_near(1)
+    w_ring(2)
+    w_fwd(0)
+    kv(2, 0).wait_recv()
+    kv(2, 1).wait_recv()
+
     def first(hp):
         @pl.when(hp == 0)
         def _():
@@ -257,97 +259,124 @@
 
         @pl.when(hp == 1)
         def _():
+            w_ring(3)
+
+        @pl.when(hp == 2)
+        def _():
             kv_far(0)
-            w_ring(3)
+            w_fwd(2)
+            w_come(FWD, 0).wait_recv()
+            w_send(FWD, 1).start()
+            w_send(SHARE + FWD, 0).start()
+
+    def second(hp):
+        @pl.when(hp == 0)
+        def _():
+            w_fwd(3)
+
+        @pl.when(hp == 1)
+        def _():
+            w_come(FWD, 1).wait_recv()
+            w_send(FWD, 2).start()
+            w_send(SHARE + FWD, 1).start()
 
         @pl.when(hp == 2)
         def _():
-            w_share(0)
-            w_fwd(2)
-
-    attention(0, first)
+            w_come(PLUS, 0).wait_recv()
+            w_send(PLUS, 1).start()
+            w_send(PLUS, 3).start()
+            w_send(PLUS, 2).start()
+            w_send(SHARE + PLUS, 0).start()
+
+    attention(1, first)
     kv_far(1)
-    for half in range(2):
-        for s in range(4):
-            w_send(PLUS, half, s).start()
-    w_fwd(3)
-    w_share(1)
+    w_send(PLUS, 0).start()
+    w_send(FWD, 3).start()
     for part in range(2):
         kv(3, part).wait_recv()
-    attention(1, lambda hp: None)
-
-    for b in (2, 3):
+    attention(2, second)
+
+    lo, hi = pl.ds(0, 64), pl.ds(64, 64)
+    left, right, far = (h + 3) % 4, (h + 1) % 4, (h + 2) % 4
+
+    def x_copy(g, k):
+        src, dst = (
+            (pb.at[g, far, lo], r1p.at[g]),
+            (pb.at[g, far, hi], r1m.at[g]),
+            (pb.at[g, right, hi], r2p.at[g, hi]),
+            (pb.at[g, left, lo], r2m.at[g, lo]),
+            (pb.at[g, right, lo], r2p.at[g, lo]),
+            (pb.at[g, left, hi], r2m.at[g, hi]),
+        )[k]
+        return remote(src, dst, xs.at[g, k], xr.at[g, k], (xp, xm)[k % 2])
+
+    def project(b):
+        for s in range(4):
+            w_come(SHARE + b, s).wait_recv()
+        g = (y + b) % 4
+        w = wb[:, g].reshape(512, 1024)
         for half in range(2):
-            for s in range(4):
-                w_come((RING, OWN, FWD, PLUS)[b], half, s).wait_recv()
-        w_share(b)
-    for b in range(4):
-        for half in range(2):
-            w_come(SHARE, half, b).wait_recv()
-
-    lo, hi = pl.ds(0, 256), pl.ds(256, 256)
-
-    def x_copy(i, k):
-        src, dst = (
-            (ps2.at[i, lo], r1p.at[i]),
-            (ps2.at[i, hi], r1m.at[i]),
-            (pp.at[i, hi], r2p.at[i, hi]),
-            (pm.at[i, lo], r2m.at[i, lo]),
-            (pp.at[i, lo], r2p.at[i, lo]),
-            (pm.at[i, hi], r2m.at[i, hi]),
-        )[k]
-        return remote(src, dst, xs.at[i, k], xr.at[i, k], (xp, xm)[k % 2])
-
-    def project(j, into, kinds):
-        w = wb[j].reshape(512, 1024)
-        for pair in range(2):
-            t = lax.dot_general(w, att[:, pair * 256 : pair * 256 + 256], NN, preferred_element_type=F32).astype(BF16)
-            for u in range(2):
-                into[2 * pair + u] = t[:, u * 128 : u * 128 + 128]
-                for k in kinds:
-                    x_copy(2 * pair + u, k).start()
-
-    project((h + 2) % 4, ps2, (0, 1))
-    project((h + 1) % 4, pp, (2,))
-    project((h + 3) % 4, pm, (3,))
-    project(h, po, ())
-
-    def merge(i, _):
-        x_copy(i, 0).wait_recv()
-        pp[i, lo, :] = (pp[i, lo, :].astype(F32) + r1p[i].astype(F32)).astype(BF16)
-        x_copy(i, 4).start()
-        x_copy(i, 1).wait_recv()
-        pm[i, hi, :] = (pm[i, hi, :].astype(F32) + r1m[i].astype(F32)).astype(BF16)
-        x_copy(i, 5).start()
-        return 0
-
-    lax.fori_loop(0, 4, merge, 0)
-
-    def write(i):
+            cols = slice(half * 256, half * 256 + 256)
+            t = lax.dot_general(w, att[:, cols], NN, preferred_element_type=F32).astype(BF16)
+            pb[g, :, :, cols] = t.reshape(4, 128, 256)
+        for k in range(4):
+            x_copy(g, k).start()
+
+    def merge(b):
+        g = (y + b) % 4
+        x_copy(g, 0).wait_recv()
+        pb[g, right, lo, :] = (pb[g, right, lo, :].astype(F32) + r1p[g].astype(F32)).astype(BF16)
+        x_copy(g, 4).start()
+        x_copy(g, 1).wait_recv()
+        pb[g, left, hi, :] = (pb[g, left, hi, :].astype(F32) + r1m[g].astype(F32)).astype(BF16)
+        x_copy(g, 5).start()
+
+    def write(g):
         return pltpu.make_async_copy(
-            obuf.at[i], out_hbm.at[pl.ds(pl.multiple_of(i * 128, 128), 128), :], lsem.at[4 + i]
+            obuf.at[g], out_hbm.at[:, pl.ds(pl.multiple_of(g * 128, 128), 128)], lsem.at[4 + g]
         )
 
-    def finish(i, _):
+    def finish(b):
+        g = (y + b) % 4
         for k in range(2, 6):
-            x_copy(i, k).wait_recv()
-        total = po[i].astype(F32) + r2p[i].astype(F32) + r2m[i].astype(F32)
-        obuf[i] = jnp.transpose(total).astype(BF16)
-        write(i).start()
-        for k in range(6):
-            x_copy(i, k).wait_send()
-        return 0
-
-    lax.fori_loop(0, 4, finish, 0)
-    for i in range(4):
-        write(i).wait()
+            x_copy(g, k).wait_recv()
+        total = pb[g, h].astype(F32) + r2p[g].astype(F32) + r2m[g].astype(F32)
+        obuf[g] = jnp.transpose(total).astype(BF16)
+        write(g).start()
+
+    def w_last(kind, steps):
+        for s in steps:
+            w_come(kind, s).wait_recv()
+            w_send(SHARE + kind, s).start()
+
+    project(0)
+    project(1)
+    merge(0)
+    merge(1)
+    w_last(FWD, (3, 2))
+    project(2)
+    w_last(PLUS, (1, 3, 2))
+    project(3)
+    finish(0)
+    merge(2)
+    finish(1)
+    merge(3)
     for kind in range(4):
         for part in range(2):
             kv(kind, part).wait_send()
-    for half in range(2):
-        for kind in range(5):
-            for s in range(3 if kind == RING else 4):
-                w_send(kind, half, s).wait_send()
+    for kind in range(SHARE + 4):
+        for s in range(3 if kind == RING else 4):
+            w_send(kind, s).wait_send()
+    finish(2)
+    for g in range(3):
+        for k in range(4):
+            x_copy((y + g) % 4, k).wait_send()
+    finish(3)
+    for g in range(4):
+        write(g).wait()
+    for b in range(4):
+        for k in range(4 if b < 3 else 0, 6):
+            x_copy((y + b) % 4, k).wait_send()
 
 
 def local(query_rows, key_rows, value_rows, doc_blocks, out_weight):
@@ -366,22 +395,19 @@
             pltpu.VMEM((128, 2560), BF16),
             pltpu.VMEM((4, 16, 128), BF16),
             pltpu.VMEM((4, 4, 2, 64, 1024), BF16),
-            pltpu.VMEM((2, 1536, 256), F32),
+            pltpu.VMEM((2, 1024, 256), F32),
             pltpu.VMEM((4, 4, 8, 256), F32),
             pltpu.VMEM((4, 4, 136, 256), F32),
             pltpu.VMEM((1024, 512), BF16),
+            pltpu.VMEM((4, 4, 128, 512), BF16),
+            pltpu.VMEM((4, 64, 512), BF16),
+            pltpu.VMEM((4, 64, 512), BF16),
+            pltpu.VMEM((4, 128, 512), BF16),
+            pltpu.VMEM((4, 128, 512), BF16),
             pltpu.VMEM((4, 512, 128), BF16),
-            pltpu.VMEM((4, 512, 128), BF16),
-            pltpu.VMEM((4, 512, 128), BF16),
-            pltpu.VMEM((4, 512, 128), BF16),
-            pltpu.VMEM((4, 256, 128), BF16),
-            pltpu.VMEM((4, 256, 128), BF16),
-            pltpu.VMEM((4, 512, 128), BF16),
-            pltpu.VMEM((4, 512, 128), BF16),
-            pltpu.VMEM((4, 128, 512), BF16),
             dma((8,)),
             dma((4, 2)), dma((4, 2)),
-            dma((5, 2, 4)), dma((5, 2, 4)),
+            dma((8, 4)), dma((8, 4)),
             dma((4, 6)), dma((4, 6)),
         ],
         compiler_params=pltpu.CompilerParams(

time: 55.5 us -> 54.2 us (0.977)
  Pallas kernels: 53.5 us -> 52.1 us
    pallas_call x1, Pallas kernels: 53.5 us -> 52.1 us  [local(): pl.pallas_call(kernel, out_shape=jax.ShapeDtypeStruct((512, 512), BF16),...]
where the time goes in v3:
time: 54.2 us; the launch traced here: 54 us
  Pallas kernels  52.1 us (96%)
  local copies, waits for them, and re-layouts  1.87 us (3%)
    pallas_call x1, Pallas kernels, local(): pl.pallas_call(kernel, out_shape=jax.ShapeDtypeStruct((512, 512), BF16),...  52.1 us
    unnamed x1, local copies, waits for them, and re-layouts  1.87 us

profile of v3, /device:TPU:1, one launch (start us, length us, event | category | flops | bytes accessed | tf_op | source)
XLA Modules:
  0.0 54.0 jit_solution(7725703303098033084)
XLA Ops:
  0.0 52.1 %shard_map.55 = bf16[512,512]{1,0:T(8,128)(2,1)} custom-call(bf16[512,1024]{1,0:T(8,128)(2,1)} %q_hbm.1, bf16[512,128]{1,0:T(8,128)(2,1)} %k_hbm.1, bf16[512,128]{1,0:T(8,128)(2,1)} %v_hbm.1, s32[16]{0:T(128)} %doc_ref.1, bf16[64,1024]{1,0:T(8,128)(2,1)} %bitcast.1), custom_call_target="tpu_custom_call" | custom-call | tf_op jit(solution)/shard_map/pallas_call | solution.py:385
  52.1 1.9 %copy.7 = bf16[512,512]{1,0:T(8,128)(2,1)} copy(bf16[512,512]{1,0:T(8,128)(2,1)} %shard_map.55) | data formatting | bytes 1048576

commit v4 on v3

--- a/solution.py
+++ b/solution.py
@@ -351,11 +351,11 @@
 
     project(0)
     project(1)
+    w_last(FWD, (3, 2))
+    w_last(PLUS, (1, 3, 2))
     merge(0)
     merge(1)
-    w_last(FWD, (3, 2))
     project(2)
-    w_last(PLUS, (1, 3, 2))
     project(3)
     finish(0)
     merge(2)

time: 54.2 us -> 52.7 us (0.972); the launches traced: 54 us -> 51.8 us
  Pallas kernels: 52.1 us -> 49.9 us
    pallas_call x1, Pallas kernels: 52.1 us -> 49.9 us  [local(): pl.pallas_call(kernel, out_shape=jax.ShapeDtypeStruct((512, 512), BF16),...]
where the time goes in v4:
time: 52.7 us; the launch traced here: 51.8 us
  Pallas kernels  49.9 us (95%)
  local copies, waits for them, and re-layouts  1.87 us (4%)
    pallas_call x1, Pallas kernels, local(): pl.pallas_call(kernel, out_shape=jax.ShapeDtypeStruct((512, 512), BF16),...  49.9 us
    unnamed x1, local copies, waits for them, and re-layouts  1.87 us

profile of v4, /device:TPU:1, one launch (start us, length us, event | category | flops | bytes accessed | tf_op | source)
XLA Modules:
  0.0 51.8 jit_solution(11269369248566075996)
XLA Ops:
  0.0 49.9 %shard_map.55 = bf16[512,512]{1,0:T(8,128)(2,1)} custom-call(bf16[512,1024]{1,0:T(8,128)(2,1)} %q_hbm.1, bf16[512,128]{1,0:T(8,128)(2,1)} %k_hbm.1, bf16[512,128]{1,0:T(8,128)(2,1)} %v_hbm.1, s32[16]{0:T(128)} %doc_ref.1, bf16[64,1024]{1,0:T(8,128)(2,1)} %bitcast.1), custom_call_target="tpu_custom_call" | custom-call | tf_op jit(solution)/shard_map/pallas_call | solution.py:385
  49.9 1.9 %copy.7 = bf16[512,512]{1,0:T(8,128)(2,1)} copy(bf16[512,512]{1,0:T(8,128)(2,1)} %shard_map.55) | data formatting | bytes 1048576

commit v5 on v4

--- a/solution.py
+++ b/solution.py
@@ -280,14 +280,6 @@
             w_send(FWD, 2).start()
             w_send(SHARE + FWD, 1).start()
 
-        @pl.when(hp == 2)
-        def _():
-            w_come(PLUS, 0).wait_recv()
-            w_send(PLUS, 1).start()
-            w_send(PLUS, 3).start()
-            w_send(PLUS, 2).start()
-            w_send(SHARE + PLUS, 0).start()
-
     attention(1, first)
     kv_far(1)
     w_send(PLUS, 0).start()
@@ -295,6 +287,11 @@
     for part in range(2):
         kv(3, part).wait_recv()
     attention(2, second)
+    w_come(PLUS, 0).wait_recv()
+    w_send(PLUS, 1).start()
+    w_send(PLUS, 3).start()
+    w_send(PLUS, 2).start()
+    w_send(SHARE + PLUS, 0).start()
 
     lo, hi = pl.ds(0, 64), pl.ds(64, 64)
     left, right, far = (h + 3) % 4, (h + 1) % 4, (h + 2) % 4

time: 52.7 us -> 52.7 us (level)
  the two profiles are of different devices: /device:TPU:1 before, /device:TPU:2 now
where the time goes in v5:
time: 52.7 us; the launch traced here: 52.6 us
  Pallas kernels  50.7 us (96%)
  local copies, waits for them, and re-layouts  1.87 us (4%)
    pallas_call x1, Pallas kernels, local(): pl.pallas_call(kernel, out_shape=jax.ShapeDtypeStruct((512, 512), BF16),...  50.7 us
    unnamed x1, local copies, waits for them, and re-layouts  1.87 us

profile of v5, /device:TPU:2, one launch (start us, length us, event | category | flops | bytes accessed | tf_op | source)
XLA Modules:
  0.0 52.6 jit_solution(11225314851651288238)
XLA Ops:
  0.0 50.7 %shard_map.55 = bf16[512,512]{1,0:T(8,128)(2,1)} custom-call(bf16[512,1024]{1,0:T(8,128)(2,1)} %q_hbm.1, bf16[512,128]{1,0:T(8,128)(2,1)} %k_hbm.1, bf16[512,128]{1,0:T(8,128)(2,1)} %v_hbm.1, s32[16]{0:T(128)} %doc_ref.1, bf16[64,1024]{1,0:T(8,128)(2,1)} %bitcast.1), custom_call_target="tpu_custom_call" | custom-call | tf_op jit(solution)/shard_map/pallas_call | solution.py:382
  50.7 1.9 %copy.7 = bf16[512,512]{1,0:T(8,128)(2,1)} copy(bf16[512,512]{1,0:T(8,128)(2,1)} %shard_map.55) | data formatting | bytes 1048576
